TPU v7x, 32 devices: a whole 2x2x4 slice. The times are simulated.
32 devices in a mesh: groups: 2 (over x), tok: 16 (over z, y, core).
Axes of the slice: x: 2, y: 2, z: 4, core: 2. Of those that a mesh axis runs over, the one named last changes fastest.
Arguments:
- activations: bfloat16 [4096, 4096], P(('groups', 'tok')), parts along dimension 0, may hold values from -6 to 6
- out_grads: bfloat16 [4096, 14336], P(('groups', 'tok')), parts along dimension 0, may hold values from -6 to 6
- query_grad: bfloat16 [8192, 14336], P(('groups', 'tok')), parts along dimension 0, may hold values from -0.00024414062 to 0.00024414062
- token_order: int32 [4096], P('groups'), parts along dimension 0, may hold values from 0 to 2047, each once
- doc_ids: int32 [4096], P('groups'), parts along dimension 0, may hold values from 0 to 31, never falling along the last dimension, each value on 1 to 128 neighbouring positions
Outputs:
- scores: float32 [64], P(('groups', 'tok')), parts along dimension 0
There are 2 independent parts, one for each index of `groups`. A program takes and returns all parts, laid end to end along the dimension named above; each array names one. Nothing has to cross between parts.
All inputs are finite; a program needn't handle non-finite values.
Results may differ from a plain program's by a relative error of at most 0.0003.
Values may be sent and summed in bfloat16 or wider, within the bound.
A program may use at most 128 MiB of HBM per device.

v0:
```python
import jax
import jax.numpy as jnp
from jax import lax
from jax.sharding import PartitionSpec as P

E_DEV = 2


def from_partner(array, axis, bit):
    return lax.ppermute(array, axis, [(i, i ^ 1 << bit) for i in range(lax.axis_size(axis))])


def shifted(value, axis, steps):
    count = lax.axis_size(axis)
    pairs = [(source, (source + steps) % count) for source in range(count)]
    return lax.ppermute(value, axis, pairs)


def order_rows(own_rows, other_rows, own_bit):
    lower_half = jnp.where(own_bit == 0, own_rows, other_rows)
    higher = jnp.where(own_bit == 0, other_rows, own_rows)
    return jnp.concatenate([lower_half, higher], axis=0)


def halve_columns(members, lower_bits, position):
    for bit_number in range(lower_bits):
        own_bit = position >> bit_number & 1
        retained = []
        outgoing = []
        for member in members:
            half_width = member.shape[1] // 2
            retained.append(lax.dynamic_slice_in_dim(member, own_bit * half_width, half_width, 1))
            outgoing.append(
                lax.dynamic_slice_in_dim(member, (1 - own_bit) * half_width, half_width, 1)
            )
        arrived = from_partner((outgoing[0], outgoing[1]), "tok", bit_number)
        members = (
            order_rows(retained[0], arrived[0], own_bit),
            order_rows(retained[1], arrived[1], own_bit),
        )
    return members


def double_rows(activations, lower_bits, position):
    for bit_number in range(lower_bits):
        own_bit = position >> bit_number & 1
        arrived = from_partner(activations, "tok", bit_number)
        activations = order_rows(activations, arrived, own_bit)
    return activations


def per_device(activations, out_grads, query_grad, token_order, doc_ids):
    axis_devices = lax.axis_size("tok")
    position = lax.axis_index("tok")
    lower_bits = 3
    window_size = 2**lower_bits
    group_count = axis_devices // window_size
    own_group = position // window_size
    query_rows, grad_rows = halve_columns((query_grad, out_grads), lower_bits, position)
    shared = double_rows(activations, lower_bits, position)
    block_rows = query_rows.shape[0]

    def accumulate(running, query_piece, first_group):
        row_start = first_group * block_rows
        columns = lax.dynamic_slice_in_dim(shared, row_start, query_piece.shape[0], 1)
        return running + jnp.dot(columns, query_piece, preferred_element_type=jnp.float32)

    running = accumulate(
        jnp.zeros((shared.shape[0], query_rows.shape[1]), jnp.float32), query_rows, own_group
    )

    def turn_single(turn_index, carried):
        partial_sum, query_piece = carried
        query_piece = shifted(query_piece, "tok", window_size)
        source = (own_group - turn_index - 1) % group_count
        return (accumulate(partial_sum, query_piece, source), query_piece)

    running, unused_piece = lax.fori_loop(0, group_count - 1, turn_single, (running, query_rows))
    partial_value = jnp.sum(running * grad_rows.astype(jnp.float32), axis=1)
    window_tokens = shared.shape[0]
    stored_order = lax.dynamic_slice_in_dim(
        token_order, own_group * window_tokens, window_tokens, 0
    )
    example_of = jnp.take(doc_ids, stored_order)
    example_count = E_DEV * axis_devices
    onehot = (example_of[:, None] == jnp.arange(example_count, dtype=jnp.int32)[None, :]).astype(
        jnp.float32
    )
    example_sums = jnp.dot(partial_value, onehot, precision=lax.Precision.HIGHEST)
    return lax.psum_scatter(example_sums, "tok", scatter_dimension=0, tiled=True)


def solution(mesh):
    placed = (
        P(("groups", "tok"), None),
        P(("groups", "tok"), None),
        P(("groups", "tok"), None),
        P("groups"),
        P("groups"),
    )
    return jax.shard_map(
        per_device, mesh=mesh, in_specs=placed, out_specs=P(("groups", "tok")), check_vma=False
    )
```

profile of v0, /device:TPU:0, one launch (start us, length us, event | category | flops | bytes accessed | tf_op | source)
XLA Modules:
  0.0 584.8 jit_solution(13418084130206135780)
XLA Ops:
  0.0 4.1 constant_dynamic-slice_fusion.1
  4.5 6.4 %collective-permute-done.3 = bf16[256,7168]{1,0:T(8,128)(2,1)} collective-permute-done((bf16[256,7168]{1,0:T(8,128)(2,1)}, bf16[256,7168]{1,0:T(8,128)(2,1)}, u32[]{:S(2)}, u32[]{:S(2)}) %collective-permute-start.3) | collective-permute-done | bytes 3670048 | tf_op jit(solution)/shard_map/ppermute | solution.py:10
  10.9 4.8 broadcast_select_fusion.2
  15.7 2.1 fusion.8
  19.8 2.9 collective-permute-start.4
  22.7 79.9 %collective-permute-done.4 = bf16[512,3584]{1,0:T(8,128)(2,1)} collective-permute-done((bf16[512,3584]{1,0:T(8,128)(2,1)}, bf16[512,3584]{1,0:T(8,128)(2,1)}, u32[]{:S(2)}, u32[]{:S(2)}) %collective-permute-start.4) | collective-permute-done | bytes 3670048 | tf_op jit(solution)/shard_map/ppermute | solution.py:10
  102.6 5.2 broadcast_select_fusion.4
  107.8 2.1 fusion.6
  119.8 3.0 broadcast_select_fusion.10
  122.8 71.1 %collective-permute-done.5 = bf16[1024,1792]{1,0:T(8,128)(2,1)} collective-permute-done((bf16[1024,1792]{1,0:T(8,128)(2,1)}, bf16[1024,1792]{1,0:T(8,128)(2,1)}, u32[]{:S(2)}, u32[]{:S(2)}) %collective-permute-start.5) | collective-permute-done | bytes 3670048 | tf_op jit(solution)/shard_map/ppermute | solution.py:10
  193.9 5.3 broadcast_select_fusion.7
  199.2 6.7 %pad_maximum_fusion = bf16[2048,1792]{1,0:T(8,128)(2,1)} fusion(bf16[1024,1792]{1,0:T(8,128)(2,1)} %get-tuple-element.16, bf16[1024,1792]{1,0:T(8,128)(2,1)} %get-tuple-element.15), kind=kLoop, calls=%fused_computation.13 | loop fusion | flops 14680064 | bytes 14680064 | tf_op jit(solution)/shard_map/concatenate | solution.py:22
  205.8 2.5 collective-permute-start.6
  210.0 2.5 broadcast_select_fusion.9
  212.6 2.5 pad_maximum_fusion.1
  217.3 31.3 %collective-permute-done.8 = bf16[256,3584]{1,0:T(8,128)(2,1)S(1)} collective-permute-done((bf16[256,3584]{1,0:T(8,128)(2,1)S(1)}, bf16[256,3584]{1,0:T(8,128)(2,1)S(1)}, u32[]{:S(2)}, u32[]{:S(2)}) %collective-permute-start.8) | collective-permute-done | bytes 1835040 | tf_op jit(solution)/shard_map/ppermute | solution.py:10
  253.3 6.2 %gather_fusion = s32[1024]{0:T(1024)S(1)} fusion(s32[2048]{0:T(1024)S(1)} %copy-done, s32[1024]{0:T(1024)S(1)} %fusion.19), kind=kCustom, calls=%fused_computation | custom fusion | bytes 12288 | tf_op jit(solution)/shard_map/jit(_take)/gather | solution.py:84
  260.8 232.9 %collective-permute-done.9 = bf16[512,1792]{1,0:T(8,128)(2,1)} collective-permute-done((bf16[512,1792]{1,0:T(8,128)(2,1)}, bf16[512,1792]{1,0:T(8,128)(2,1)}, u32[]{:S(2)}, u32[]{:S(2)}) %collective-permute-start.9) | collective-permute-done | bytes 1835040 | tf_op jit(solution)/shard_map/ppermute | solution.py:10
  493.7 3.0 broadcast_select_fusion.15
  496.7 3.6 broadcast_select_fusion
  500.3 22.6 %collective-permute-done.6 = bf16[2048,1792]{1,0:T(8,128)(2,1)} collective-permute-done((bf16[2048,1792]{1,0:T(8,128)(2,1)}, bf16[2048,1792]{1,0:T(8,128)(2,1)}, u32[]{:S(2)}, u32[]{:S(2)}) %collective-permute-start.6) | collective-permute-done | bytes 7340064 | tf_op jit(solution)/shard_map/while/body/eval_jaxpr/ppermute | solution.py:16
  523.0 14.6 %fusion.1 = f32[1024,1792]{1,0:T(8,128)} fusion(bf16[2048,1792]{1,0:T(8,128)(2,1)} %collective-permute-done.6, s32[]{:T(128)S(6)} %select_n.193, bf16[512,4096]{1,0:T(8,128)(2,1)S(1)} %get-tuple-element.30, bf16[512,4096]{1,0:T(8,128)(2,1)S(1)} %get-tuple-element.29), kind=kOutput, calls=%fused_computation.16 | convolution fusion | flops 7524581376 | bytes 23068676 | tf_op jit(solution)/shard_map/while/body/eval_jaxpr/dot_general | solution.py:66
  537.6 13.1 %multiply_reduce_fusion = f32[1024]{0:T(1024)S(1)} fusion(f32[1024,1792]{1,0:T(8,128)} %fusion.1, bf16[512,1792]{1,0:T(8,128)(2,1)S(1)} %get-tuple-element.32, bf16[512,1792]{1,0:T(8,128)(2,1)S(1)} %get-tuple-element.31, s32[]{:T(128)S(6)} %select_n.176, bf16[512,4096]{1,0:T(8,128)(2,1)} %copy-done.21, bf16[512,4096]{1,0:T(8,128)(2,1)} %copy-done.20, ...), kind=kOutput, calls=%fused_computation.14 | convolution fusion | flops 7552105472 | bytes 26742788 | tf_op jit(solution)/shard_map/dot_general | solution.py:66
  551.1 33.1 %all-reduce = f32[32]{0:T(128)S(1)} all-reduce(f32[32]{0:T(128)S(1)} %convolution_bitcast_fusion), channel_id=2, replica_groups=mesh['groups'=2,'tok'=16] {'tok'}, use_global_device_ids=true, to_apply=%region_1.2.clone | all-reduce | flops 32 | bytes 256
  (77 shorter events, 22.3 us)
Async XLA Ops:
  0.0 253.3 %copy-start = (s32[2048]{0:T(1024)S(1)}, s32[2048]{0:T(1024)}, u32[]{:S(2)}) copy-start(s32[2048]{0:T(1024)} %param.9) | copy-start | bytes 24580
  4.1 6.8 %collective-permute-start.3 = (bf16[256,7168]{1,0:T(8,128)(2,1)}, bf16[256,7168]{1,0:T(8,128)(2,1)}, u32[]{:S(2)}, u32[]{:S(2)}) collective-permute-start(bf16[256,7168]{1,0:T(8,128)(2,1)} %constant_dynamic-slice_fusion.1), channel_id=1, source_target_pairs={{0,1},{1,0},{2,3},{3,2},{4,5},{5,4},{6,7},{7,6},{8,9},{9,8},{10,11... | collective-permute-start | bytes 11010056 | tf_op jit(solution)/shard_map/ppermute | solution.py:10
  19.8 82.8 %collective-permute-start.4 = (bf16[512,3584]{1,0:T(8,128)(2,1)}, bf16[512,3584]{1,0:T(8,128)(2,1)}, u32[]{:S(2)}, u32[]{:S(2)}) collective-permute-start(bf16[512,3584]{1,0:T(8,128)(2,1)} %fusion.8), channel_id=1, source_target_pairs={{0,2},{1,3},{2,0},{3,1},{4,6},{5,7},{6,4},{7,5},{8,10},{9,11},{10,... | collective-permute-start | bytes 11010056 | tf_op jit(solution)/shard_map/ppermute | solution.py:10
  22.7 92.1 %collective-permute-start = (bf16[128,4096]{1,0:T(8,128)(2,1)S(1)}, bf16[128,4096]{1,0:T(8,128)(2,1)}, u32[]{:S(2)}, u32[]{:S(2)}) collective-permute-start(bf16[128,4096]{1,0:T(8,128)(2,1)S(1)} %copy-done.24), channel_id=1, source_target_pairs={{0,1},{1,0},{2,3},{3,2},{4,5},{5,4},{6,7},{7,6},{8,9},{9,8},{10,11... | collective-permute-start | bytes 3145736 | tf_op jit(solution)/shard_map/ppermute | solution.py:10
  112.7 81.2 %collective-permute-start.5 = (bf16[1024,1792]{1,0:T(8,128)(2,1)}, bf16[1024,1792]{1,0:T(8,128)(2,1)}, u32[]{:S(2)}, u32[]{:S(2)}) collective-permute-start(bf16[1024,1792]{1,0:T(8,128)(2,1)} %fusion.6), channel_id=1, source_target_pairs={{0,4},{1,5},{2,6},{3,7},{4,0},{5,1},{6,2},{7,3},{8,12},{9,13},{10,... | collective-permute-start | bytes 11010056 | tf_op jit(solution)/shard_map/ppermute | solution.py:10
  114.7 5.2 collective-permute-start.7
  118.3 75.6 %copy-start.3 = (bf16[512,3584]{1,0:T(8,128)(2,1)S(1)}, bf16[512,3584]{1,0:T(8,128)(2,1)}, u32[]{:S(2)}) copy-start(bf16[512,3584]{1,0:T(8,128)(2,1)} %copy-done.2) | copy-start | bytes 11010052
  118.3 75.6 %copy-start.5 = (bf16[512,3584]{1,0:T(8,128)(2,1)S(1)}, bf16[512,3584]{1,0:T(8,128)(2,1)}, u32[]{:S(2)}) copy-start(bf16[512,3584]{1,0:T(8,128)(2,1)} %copy-done.4) | copy-start | bytes 11010052
  118.3 91.7 %collective-permute-start.1 = (bf16[256,4096]{1,0:T(8,128)(2,1)}, bf16[256,4096]{1,0:T(8,128)(2,1)}, u32[]{:S(2)}, u32[]{:S(2)}) collective-permute-start(bf16[256,4096]{1,0:T(8,128)(2,1)} %pad_maximum_fusion.2), channel_id=1, source_target_pairs={{0,2},{1,3},{2,0},{3,1},{4,6},{5,7},{6,4},{7,5},{8,10},{9,11},{10,... | collective-permute-start | bytes 6291464 | tf_op jit(solution)/shard_map/ppermute | solution.py:10
  122.8 85.5 %copy-start.12 = (bf16[128,7168]{1,0:T(8,128)(2,1)}, bf16[128,7168]{1,0:T(8,128)(2,1)S(1)}, u32[]{:S(2)}) copy-start(bf16[128,7168]{1,0:T(8,128)(2,1)S(1)} %get-tuple-element.35) | copy-start | bytes 5505028
  122.8 85.5 %copy-start.14 = (bf16[128,7168]{1,0:T(8,128)(2,1)}, bf16[128,7168]{1,0:T(8,128)(2,1)S(1)}, u32[]{:S(2)}) copy-start(bf16[128,7168]{1,0:T(8,128)(2,1)S(1)} %get-tuple-element.36) | copy-start | bytes 5505028
  205.8 317.1 %collective-permute-start.6 = (bf16[2048,1792]{1,0:T(8,128)(2,1)}, bf16[2048,1792]{1,0:T(8,128)(2,1)}, u32[]{:S(2)}, u32[]{:S(2)}) collective-permute-start(bf16[2048,1792]{1,0:T(8,128)(2,1)} %pad_maximum_fusion), channel_id=1, source_target_pairs={{0,8},{1,9},{2,10},{3,11},{4,12},{5,13},{6,14},{7,15},{8,0},{9,1},... | collective-permute-start | bytes 22020104 | tf_op jit(solution)/shard_map/while/body/eval_jaxpr/ppermute | solution.py:16
  208.5 40.1 %collective-permute-start.8 = (bf16[256,3584]{1,0:T(8,128)(2,1)S(1)}, bf16[256,3584]{1,0:T(8,128)(2,1)S(1)}, u32[]{:S(2)}, u32[]{:S(2)}) collective-permute-start(bf16[256,3584]{1,0:T(8,128)(2,1)S(1)} %fusion.12), channel_id=1, source_target_pairs={{0,2},{1,3},{2,0},{3,1},{4,6},{5,7},{6,4},{7,5},{8,10},{9,11},{10,... | collective-permute-start | bytes 5505032 | tf_op jit(solution)/shard_map/ppermute | solution.py:10
  212.6 36.0 %copy-start.13 = (bf16[128,7168]{1,0:T(8,128)(2,1)S(1)}, bf16[128,7168]{1,0:T(8,128)(2,1)}, u32[]{:S(2)}) copy-start(bf16[128,7168]{1,0:T(8,128)(2,1)} %copy-done.12) | copy-start | bytes 5505028
  212.6 36.0 %copy-start.15 = (bf16[128,7168]{1,0:T(8,128)(2,1)S(1)}, bf16[128,7168]{1,0:T(8,128)(2,1)}, u32[]{:S(2)}) copy-start(bf16[128,7168]{1,0:T(8,128)(2,1)} %copy-done.14) | copy-start | bytes 5505028
  215.8 280.9 %collective-permute-start.2 = (bf16[512,4096]{1,0:T(8,128)(2,1)}, bf16[512,4096]{1,0:T(8,128)(2,1)}, u32[]{:S(2)}, u32[]{:S(2)}) collective-permute-start(bf16[512,4096]{1,0:T(8,128)(2,1)} %pad_maximum_fusion.1), channel_id=1, source_target_pairs={{0,4},{1,5},{2,6},{3,7},{4,0},{5,1},{6,2},{7,3},{8,12},{9,13},{10,... | collective-permute-start | bytes 12582920 | tf_op jit(solution)/shard_map/ppermute | solution.py:10
  250.5 9.0 %copy-start.26 = (u32[32]{0:T(128)S(1)}, u32[32]{0:T(128)}, u32[]{:S(2)}) copy-start(u32[32]{0:T(128)} %constant.77) | copy-start | bytes 388
  251.8 241.9 %collective-permute-start.9 = (bf16[512,1792]{1,0:T(8,128)(2,1)}, bf16[512,1792]{1,0:T(8,128)(2,1)}, u32[]{:S(2)}, u32[]{:S(2)}) collective-permute-start(bf16[512,1792]{1,0:T(8,128)(2,1)} %fusion.10), channel_id=1, source_target_pairs={{0,4},{1,5},{2,6},{3,7},{4,0},{5,1},{6,2},{7,3},{8,12},{9,13},{10,... | collective-permute-start | bytes 5505032 | tf_op jit(solution)/shard_map/ppermute | solution.py:10
  260.8 235.9 %copy-start.9 = (bf16[256,4096]{1,0:T(8,128)(2,1)S(1)}, bf16[256,4096]{1,0:T(8,128)(2,1)}, u32[]{:S(2)}) copy-start(bf16[256,4096]{1,0:T(8,128)(2,1)} %copy-done.8) | copy-start | bytes 6291460
  500.3 37.3 %copy-start.20 = (bf16[512,4096]{1,0:T(8,128)(2,1)}, bf16[512,4096]{1,0:T(8,128)(2,1)S(1)}, u32[]{:S(2)}) copy-start(bf16[512,4096]{1,0:T(8,128)(2,1)S(1)} %get-tuple-element.29) | copy-start | bytes 12582916
  500.3 37.3 %copy-start.21 = (bf16[512,4096]{1,0:T(8,128)(2,1)}, bf16[512,4096]{1,0:T(8,128)(2,1)S(1)}, u32[]{:S(2)}) copy-start(bf16[512,4096]{1,0:T(8,128)(2,1)S(1)} %get-tuple-element.30) | copy-start | bytes 12582916
  523.0 14.7 %copy-start.16 = (bf16[1024,1792]{1,0:T(8,128)(2,1)S(1)}, bf16[1024,1792]{1,0:T(8,128)(2,1)}, u32[]{:S(2)}) copy-start(bf16[1024,1792]{1,0:T(8,128)(2,1)} %get-tuple-element.15) | copy-start | bytes 11010052
  523.0 14.7 %copy-start.17 = (bf16[1024,1792]{1,0:T(8,128)(2,1)S(1)}, bf16[1024,1792]{1,0:T(8,128)(2,1)}, u32[]{:S(2)}) copy-start(bf16[1024,1792]{1,0:T(8,128)(2,1)} %get-tuple-element.16) | copy-start | bytes 11010052
  537.6 47.2 %copy-start.1 = (s32[2048]{0:T(1024)S(1)}, s32[2048]{0:T(1024)}, u32[]{:S(2)}) copy-start(s32[2048]{0:T(1024)} %param.9) | copy-start | bytes 24580
  (13 other events, 52.8 us)
where the time goes:
time: 585 us
  waiting for transfers between devices  444 us (76%)
  other arithmetic  46.5 us (8%)
  blocking collectives  33.1 us (6%)
  matrix products  28.1 us (5%)
  local copies, waits for them, and re-layouts  18.1 us (3%)
  starting transfers between devices  13.8 us (2%)
    ppermute x9, waiting for transfers between devices, from_partner(): lax.ppermute(array, axis, [(i, i ^ 1 << bit) for i in range(lax.axis_size...  422 us
    unnamed x1, blocking collectives  33.1 us
    dot_general x2, matrix products, accumulate(): jnp.dot(columns, query_piece, preferred_element_type=jnp.float32)  27.7 us
    ppermute x1, waiting for transfers between devices, shifted(): return lax.ppermute(value, axis, pairs)  22.6 us
    select_n x5, other arithmetic, order_rows(): higher = jnp.where(own_bit == 0, other_rows, own_rows)  17.2 us
    concatenate x7, other arithmetic, order_rows(): return jnp.concatenate([lower_half, higher], axis=0)  16.6 us
    select_n x4, other arithmetic, order_rows(): lower_half = jnp.where(own_bit == 0, own_rows, other_rows)  12.6 us
  transfers between devices with their start and end apart: 10, of which 6 were waited for; matrix products, arithmetic and copies ran while one was open for 8% of the time, Pallas kernels for 0%

commit v1 on v0

--- a/solution.py
+++ b/solution.py
@@ -1,9 +1,272 @@
+import functools
+
 import jax
 import jax.numpy as jnp
 from jax import lax
+from jax.experimental import pallas as pl
+from jax.experimental.pallas import tpu as pltpu
 from jax.sharding import PartitionSpec as P
 
 E_DEV = 2
+ROW = 4
+LINE = 4
+MESH = pl.DeviceIdType.MESH
+NEED = ((0,), (0, 1), (2, 3), (3,))
+RIGHTWARD = {1: (0, 1, 2, 3), 2: (2, 3), 3: (3,)}
+LEFTWARD = {2: (0, 1, 2, 3), 1: (0, 1), 0: (0,)}
+
+
+def exchange(
+    near, act, grads, query, g_all, a_all, q_own, q_next,
+    g_recv, a_recv, q_recv, n_recv, row_send, right_a, right_b, left_a, left_b, act_right, act_left,
+    act_row, q_send,
+):
+    me = lax.axis_index("tok")
+    z = me // ROW
+    s = me % ROW
+    y, c = s // 2, s % 2
+    tokens, features = act.shape
+    q_rows = query.shape[0]
+    width = g_all.shape[1]
+    far = width - near
+    block = features // LINE
+    core_peer = y * 2 + 1 - c
+    y_peer = (1 - y) * 2 + c
+    diagonal = (1 - y) * 2 + 1 - c
+    peers = (s, core_peer, y_peer, diagonal)
+
+    barrier = pltpu.get_barrier_semaphore()
+    for step in range(1, ROW * LINE):
+        other = (me + step) % (ROW * LINE)
+        pl.semaphore_signal(barrier, inc=1, device_id={"tok": other}, device_id_type=MESH)
+    pl.semaphore_wait(barrier, ROW * LINE - 1)
+
+    def remote(source, target, send, recv, line, quarter):
+        return pltpu.make_async_remote_copy(
+            src_ref=source, dst_ref=target, send_sem=send, recv_sem=recv,
+            device_id={"tok": line * ROW + quarter}, device_id_type=MESH,
+        )
+
+    def rows(line, quarter):
+        return pl.ds(pl.multiple_of((line * ROW + quarter) * tokens, tokens), tokens)
+
+    def g_piece(line, quarter, piece):
+        columns = pl.ds(0, near) if piece == 0 else pl.ds(near, far)
+        return g_all.at[rows(line, quarter), columns]
+
+    def a_piece(line, quarter, number):
+        return a_all.at[rows(line, quarter), pl.ds(number * block, block)]
+
+    def arrived(ref, sem):
+        pltpu.make_async_copy(ref, ref, sem).wait()
+
+    def role(zz):
+        inner = zz in (1, 2)
+        mate = {0: 1, 1: 2, 2: 1, 3: 2}[zz]
+
+        def g_wait(line, quarter, piece):
+            arrived(g_piece(line, quarter, piece), g_recv.at[line, quarter, piece])
+
+        def g_forward(line, quarter, piece, target, send):
+            ref = g_piece(line, quarter, piece)
+            remote(ref, ref, send, g_recv.at[line, quarter, piece], target, s).start()
+
+        def a_wait(line, quarter, number):
+            arrived(a_piece(line, quarter, number), a_recv.at[line, quarter, number])
+
+        def a_forward(line, quarter, number, target, target_quarter, send):
+            ref = a_piece(line, quarter, number)
+            remote(ref, ref, send, a_recv.at[line, quarter, number], target, target_quarter).start()
+
+        def spread(line):
+            for number in NEED[zz]:
+                for quarter in (core_peer, y_peer):
+                    a_forward(line, s, number, zz, quarter, act_row)
+
+        def relay(line):
+            for number in NEED[zz]:
+                a_wait(line, y_peer, number)
+                a_forward(line, y_peer, number, zz, core_peer, act_row)
+
+        for place, quarter in enumerate(peers):
+            for piece in (0, 1):
+                start = quarter * width + piece * near
+                size = far if piece else near
+                source = grads.at[:, pl.ds(pl.multiple_of(start, 128), size)]
+                target = g_piece(zz, s, piece)
+                sem = g_recv.at[zz, s, piece]
+                if piece and not inner:
+                    remote(source, target, row_send, sem, mate, quarter).start()
+                elif place == 0:
+                    pltpu.make_async_copy(source, target, sem).start()
+                else:
+                    remote(source, target, row_send, sem, zz, quarter).start()
+        for number in NEED[zz]:
+            own = act.at[:, pl.ds(number * block, block)]
+            pltpu.make_async_copy(own, a_piece(zz, s, number), a_recv.at[zz, s, number]).start()
+        for target, numbers, send in (
+            (zz + 1, RIGHTWARD.get(zz + 1, ()), act_right), (zz - 1, LEFTWARD.get(zz - 1, ()), act_left),
+        ):
+            for number in numbers:
+                own = act.at[:, pl.ds(number * block, block)]
+                sem = a_recv.at[zz, s, number]
+                remote(own, a_piece(zz, s, number), send, sem, target, s).start()
+
+        for quarter in peers:
+            g_wait(zz, quarter, 0)
+            if zz < LINE - 1:
+                g_forward(zz, quarter, 0, zz + 1, right_a)
+            if zz > 0:
+                g_forward(zz, quarter, 0, zz - 1, left_a)
+            if inner:
+                g_wait(zz, quarter, 1)
+                g_forward(zz, quarter, 1, mate, right_b if zz == 1 else left_b)
+
+        for place, quarter in enumerate(peers):
+            start = pl.multiple_of(quarter * width, 128)
+            held = pl.ds(pl.multiple_of(s * q_rows, q_rows), q_rows)
+            size = width if inner else near
+            source = query.at[:, pl.ds(start, size)]
+            target = q_own.at[held, pl.ds(0, size)]
+            if place == 0:
+                pltpu.make_async_copy(source, target, q_recv.at[s]).start()
+            else:
+                remote(source, target, q_send, q_recv.at[s], zz, quarter).start()
+            if not inner:
+                source = query.at[:, pl.ds(pl.multiple_of(start + near, 128), far)]
+                remote(source, q_next.at[held, :], q_send, n_recv.at[s], mate, quarter).start()
+        for number in NEED[zz]:
+            a_wait(zz, s, number)
+        spread(zz)
+
+        for distance in range(1, LINE):
+            from_left, from_right = zz - distance, zz + distance
+            if from_left >= 0:
+                for number in RIGHTWARD[zz]:
+                    a_wait(from_left, s, number)
+                for number in RIGHTWARD.get(zz + 1, ()):
+                    a_forward(from_left, s, number, zz + 1, s, act_right)
+                spread(from_left)
+            if from_right < LINE:
+                for number in LEFTWARD[zz]:
+                    a_wait(from_right, s, number)
+                for number in LEFTWARD.get(zz - 1, ()):
+                    a_forward(from_right, s, number, zz - 1, s, act_left)
+                spread(from_right)
+            for quarter in peers:
+                if from_left >= 0:
+                    g_wait(from_left, quarter, 0)
+                    if zz < LINE - 1:
+                        g_forward(from_left, quarter, 0, zz + 1, right_a)
+                if from_right < LINE:
+                    g_wait(from_right, quarter, 0)
+                    if zz > 0:
+                        g_forward(from_right, quarter, 0, zz - 1, left_a)
+                if inner and from_left >= 0:
+                    g_wait(from_left, quarter, 1)
+                    if zz == 1:
+                        g_forward(from_left, quarter, 1, mate, right_b)
+                if inner and from_right < LINE:
+                    g_wait(from_right, quarter, 1)
+                    if zz == 2:
+                        g_forward(from_right, quarter, 1, mate, left_b)
+            if distance == 1:
+                relay(zz)
+            if from_left >= 0:
+                relay(from_left)
+            if from_right < LINE:
+                relay(from_right)
+
+        for line in range(LINE):
+            for quarter in (core_peer, diagonal):
+                for number in NEED[zz]:
+                    a_wait(line, quarter, number)
+        for quarter in range(ROW):
+            held = pl.ds(quarter * q_rows, q_rows)
+            size = width if inner else near
+            arrived(q_own.at[held, pl.ds(0, size)], q_recv.at[quarter])
+            if inner:
+                arrived(q_next.at[held, :], n_recv.at[quarter])
+
+        sent = 3 * width if inner else 3 * width + far
+        arrived(grads.at[:, pl.ds(0, sent)], row_send)
+        arrived(query.at[:, pl.ds(0, sent)], q_send)
+        line_rows = ROW * tokens
+        if zz < LINE - 1:
+            arrived(g_all.at[pl.ds(0, (zz + 1) * line_rows), pl.ds(0, near)], right_a)
+            wide = len(RIGHTWARD[zz + 1]) * block
+            arrived(a_all.at[pl.ds(0, (zz + 1) * tokens), pl.ds(0, wide)], act_right)
+        if zz > 0:
+            arrived(g_all.at[pl.ds(0, (LINE - zz) * line_rows), pl.ds(0, near)], left_a)
+            wide = len(LEFTWARD[zz - 1]) * block
+            arrived(a_all.at[pl.ds(0, (LINE - zz) * tokens), pl.ds(0, wide)], act_left)
+        if inner:
+            half = g_all.at[pl.ds(0, 2 * line_rows), pl.ds(near, far)]
+            arrived(half, right_b if zz == 1 else left_b)
+        wide = len(NEED[zz]) * block
+        arrived(a_all.at[pl.ds(0, 3 * LINE * tokens), pl.ds(0, wide)], act_row)
+
+    for zz in range(LINE):
+        pl.when(z == zz)(functools.partial(role, zz))
+
+
+def on_line(activations, out_grads, query_grad, token_order, doc_ids):
+    tokens, features = activations.shape
+    columns = out_grads.shape[1]
+    width = columns // ROW
+    near = width * 4 // 7 // 256 * 256
+    far = width - near
+    q_rows = query_grad.shape[0]
+    count = ROW * LINE
+    block = features // LINE
+    position = lax.axis_index("tok")
+    dma = pltpu.SemaphoreType.DMA
+    g_all, a_all, q_own, q_next = pl.pallas_call(
+        functools.partial(exchange, near),
+        out_shape=(
+            jax.ShapeDtypeStruct((count * tokens, width), jnp.bfloat16),
+            jax.ShapeDtypeStruct((count * tokens, features), jnp.bfloat16),
+            jax.ShapeDtypeStruct((ROW * q_rows, width), jnp.bfloat16),
+            jax.ShapeDtypeStruct((ROW * q_rows, far), jnp.bfloat16),
+        ),
+        in_specs=[pl.BlockSpec(memory_space=pl.ANY)] * 3,
+        out_specs=[pl.BlockSpec(memory_space=pl.ANY)] * 4,
+        scratch_shapes=[
+            dma((LINE, ROW, 2)), dma((LINE, ROW, LINE)), dma((ROW,)), dma((ROW,)),
+        ] + [dma] * 9,
+        compiler_params=pltpu.CompilerParams(collective_id=0, has_side_effects=True),
+        name="exchange",
+    )(activations, out_grads, query_grad)
+
+    def end_scores(number):
+        rows_in = a_all[:, number * block : (number + 1) * block]
+        projected = jnp.dot(rows_in, q_own[:, :near], preferred_element_type=jnp.float32)
+        return jnp.sum(projected * g_all[:, :near].astype(jnp.float32), axis=1)
+
+    def inner_scores(number, mate):
+        rows_in = a_all[:, number * block : (number + 1) * block]
+        rows_mate = a_all[:, mate * block : (mate + 1) * block]
+        extra = jnp.dot(rows_in, q_own[:, near:], preferred_element_type=jnp.float32)
+        extra = extra + jnp.dot(rows_mate, q_next, preferred_element_type=jnp.float32)
+        extra = jnp.sum(extra * g_all[:, near:].astype(jnp.float32), axis=1)
+        return end_scores(number) + extra
+
+    partial_value = lax.switch(
+        position // ROW,
+        [
+            functools.partial(end_scores, 0),
+            functools.partial(inner_scores, 1, 0),
+            functools.partial(inner_scores, 2, 3),
+            functools.partial(end_scores, 3),
+        ],
+    )
+    example_of = jnp.take(doc_ids, token_order)
+    example_count = E_DEV * count
+    onehot = (example_of[:, None] == jnp.arange(example_count, dtype=jnp.int32)[None, :]).astype(
+        jnp.float32
+    )
+    example_sums = jnp.dot(partial_value, onehot, precision=lax.Precision.HIGHEST)
+    return lax.psum_scatter(example_sums, "tok", scatter_dimension=0, tiled=True)
 
 
 def from_partner(array, axis, bit):
@@ -98,6 +361,7 @@
         P("groups"),
         P("groups"),
     )
+    local = on_line if mesh.shape["tok"] == ROW * LINE else per_device
     return jax.shard_map(
-        per_device, mesh=mesh, in_specs=placed, out_specs=P(("groups", "tok")), check_vma=False
-    )
+        local, mesh=mesh, in_specs=placed, out_specs=P(("groups", "tok")), check_vma=False
+    )

time: 585 us -> 362 us (0.62)
  waiting for transfers between devices: 444 us -> 0 us
  Pallas kernels: 0 us -> 268 us
  other arithmetic: 46.5 us -> 0.01 us
  local copies, waits for them, and re-layouts: 18.1 us -> 33.3 us
  matrix products: 28.1 us -> 14.2 us
  starting transfers between devices: 13.8 us -> 0 us
  blocking collectives: 33.1 us -> 45.3 us
    ppermute x10 -> x0, waiting for transfers between devices: 444 us -> none  [the longest x9 422 us: from_partner(): lax.ppermute(array, axis, [(i, i ^ 1 << bit) for i in range(lax.axis_size...]
    pallas_call x0 -> x1, Pallas kernels: none -> 268 us  [on_line(): pl.pallas_call(functools.partial(exchange, near), out_shape=(jax.ShapeDty...]
    select_n x10 -> x1, other arithmetic: 29.8 us -> 0.01 us  [on_line(): example_of = jnp.take(doc_ids, token_order)]
    another operation x0 -> x1, local copies, waits for them, and re-layouts: none -> 20.3 us
    concatenate x7 -> x0, other arithmetic: 16.6 us -> none  [order_rows(): return jnp.concatenate([lower_half, higher], axis=0)]
    dot_general x3 -> x2, matrix products: 28.1 us -> 14.2 us  [the longest x1 13.6 us: end_scores(): jnp.dot(rows_in, q_own[:, :near], preferred_element_type=jnp.float32)]
    ppermute x10 -> x0, starting transfers between devices: 13.8 us -> none  [the longest x9 11.3 us: from_partner(): lax.ppermute(array, axis, [(i, i ^ 1 << bit) for i in range(lax.axis_size...]
    unnamed x1, blocking collectives: 33.1 us -> 45.3 us
  transfers between devices with their start and end apart: 10 -> 0, of which waited for: 6 -> 0; matrix products, arithmetic and copies ran while one was open for 8% -> 0% of each run, Pallas kernels for 0% -> 0%
where the time goes in v1:
time: 362 us
  Pallas kernels  268 us (74%)
  blocking collectives  45.3 us (13%)
  local copies, waits for them, and re-layouts  33.3 us (9%)
  matrix products  14.2 us (4%)
    pallas_call x1, Pallas kernels, on_line(): pl.pallas_call(functools.partial(exchange, near), out_shape=(jax.ShapeDty...  268 us
    unnamed x1, blocking collectives  45.3 us
    another operation x1, local copies, waits for them, and re-layouts  20.3 us
    dot_general x1, matrix products, end_scores(): jnp.dot(rows_in, q_own[:, :near], preferred_element_type=jnp.float32)  13.6 us
    gather x1, local copies, waits for them, and re-layouts, on_line(): example_of = jnp.take(doc_ids, token_order)  11.8 us

profile of v1, /device:TPU:0, one launch (start us, length us, event | category | flops | bytes accessed | tf_op | source)
XLA Modules:
  0.0 361.8 jit_solution(14217634126435945986)
XLA Ops:
  0.0 0.0 copy-start
  0.0 267.7 %exchange.1 = (bf16[2048,3584]{1,0:T(8,128)(2,1)}, bf16[2048,4096]{1,0:T(8,128)(2,1)}, bf16[1024,3584]{1,0:T(8,128)(2,1)}, bf16[1024,1536]{1,0:T(8,128)(2,1)S(1)}) custom-call(bf16[128,4096]{1,0:T(8,128)(2,1)} %act.1, bf16[128,14336]{1,0:T(8,128)(2,1)} %grads.1, bf16[256,14336]{1,0:T(8,128)(2,1)} %query.1), custom_call_target="tpu_custom_call" | custom-call | tf_op jit(solution)/shard_map/exchange/pallas_call | solution.py:224
  267.7 0.0 copy-start.1
  267.7 34.5 %conditional.1 = (f32[2048]{0:T(1024)S(1)}) conditional(s32[]{:T(128)} %clamp.3, (bf16[2048,4096]{1,0:T(8,128)(2,1)}, bf16[1024,3584]{1,0:T(8,128)(2,1)}, bf16[2048,3584]{1,0:T(8,128)(2,1)}) %tuple.17, (bf16[2048,4096]{1,0:T(8,128)(2,1)}, bf16[1024,3584]{1,0:T(8,128)(2,1)}, bf16[2048,3584]{1,0:T(8,128)(2,1)}, ...), branch_computations={%region_0.2_spmd, %region_2.5_spmd, %region_5.8_spmd, %region_8.10... | conditional | flops 21500000256 | bytes 92315656 | solution.py:254
  267.7 20.3 %copy.14 = bf16[2048,3584]{0,1:T(8,128)(2,1)} copy(bf16[2048,3584]{1,0:T(8,128)(2,1)} %get-tuple-element.90) | data formatting | bytes 29360128 | tf_op jit(solution)/shard_map
  288.0 13.6 %multiply_reduce_fusion = f32[2048]{0:T(1024)S(1)} fusion(bf16[2048,3584]{0,1:T(8,128)(2,1)} %copy.14, bf16[1024,3584]{1,0:T(8,128)(2,1)} %get-tuple-element.38, bf16[2048,4096]{1,0:T(8,128)(2,1)} %get-tuple-element.36), kind=kOutput, calls=%fused_computation.1 | convolution fusion | flops 8602515456 | bytes 16785408 | tf_op jit(solution)/shard_map/cond/branch_0_fun/dot_general | solution.py:243
  302.2 0.0 copy-start.2
  302.2 0.0 copy-done.1
  302.2 0.0 copy-done
  302.2 11.8 %gather_fusion = s32[2048]{0:T(1024)S(1)} fusion(s32[2048]{0:T(1024)S(1)} %copy-done, s32[2048]{0:T(1024)S(1)} %fusion.17), kind=kCustom, calls=%fused_computation | custom fusion | bytes 24576 | tf_op jit(solution)/shard_map/jit(_take)/gather | solution.py:263
  314.0 0.6 convolution_bitcast_fusion
  314.6 45.3 %all-reduce = f32[32]{0:T(128)S(1)} all-reduce(f32[32]{0:T(128)S(1)} %convolution_bitcast_fusion), channel_id=2, replica_groups=mesh['groups'=2,'tok'=16] {'tok'}, use_global_device_ids=true, to_apply=%region_10.11.clone | all-reduce | flops 32 | bytes 256
  360.0 0.0 copy-done.2
  360.0 0.6 dynamic-slice
  361.2 0.6 dynamic-slice.1
  (2 shorter events, 0.0 us)
Async XLA Ops:
  0.0 302.2 %copy-start = (s32[2048]{0:T(1024)S(1)}, s32[2048]{0:T(1024)}, u32[]{:S(2)}) copy-start(s32[2048]{0:T(1024)} %param.13) | copy-start | bytes 24580
  267.7 34.5 %copy-start.1 = (s32[2048]{0:T(1024)S(1)}, s32[2048]{0:T(1024)}, u32[]{:S(2)}) copy-start(s32[2048]{0:T(1024)} %param.12) | copy-start | bytes 24580
  302.2 57.8 %copy-start.2 = (u32[32]{0:T(128)S(1)}, u32[32]{0:T(128)}, u32[]{:S(2)}) copy-start(u32[32]{0:T(128)} %constant.47) | copy-start | bytes 388

commit v2 on v0

--- a/solution.py
+++ b/solution.py
@@ -1,9 +1,358 @@
+import functools
+
 import jax
 import jax.numpy as jnp
 from jax import lax
+from jax.experimental import pallas as pl
+from jax.experimental.pallas import tpu as pltpu
 from jax.sharding import PartitionSpec as P
 
 E_DEV = 2
+ROW = 4
+LINE = 4
+MESH = pl.DeviceIdType.MESH
+NEED = ((0,), (0, 1), (2, 3), (3,))
+RIGHTWARD = {1: (0, 1, 2, 3), 2: (2, 3), 3: (3,)}
+LEFTWARD = {2: (0, 1, 2, 3), 1: (0, 1), 0: (0,)}
+
+
+def exchange(
+    near, act, grads, query, member, out, g_all, a_all, q_own, q_next, total, mine, slots,
+    g_recv, a_recv, q_recv, n_recv, row_send, right_a, right_b, left_a, left_b, act_right, act_left,
+    act_row, q_send, n_send,
+    sum_recv, sum_send,
+):
+    me = lax.axis_index("tok")
+    z = me // ROW
+    s = me % ROW
+    y, c = s // 2, s % 2
+    tokens, features = act.shape
+    q_rows = query.shape[0]
+    width = g_all.shape[1]
+    far = width - near
+    block = features // LINE
+    core_peer = y * 2 + 1 - c
+    y_peer = (1 - y) * 2 + c
+    diagonal = (1 - y) * 2 + 1 - c
+    peers = (s, core_peer, y_peer, diagonal)
+
+    barrier = pltpu.get_barrier_semaphore()
+    for step in range(1, ROW * LINE):
+        other = (me + step) % (ROW * LINE)
+        pl.semaphore_signal(barrier, inc=1, device_id={"tok": other}, device_id_type=MESH)
+    pl.semaphore_wait(barrier, ROW * LINE - 1)
+
+    def remote(source, target, send, recv, line, quarter):
+        return pltpu.make_async_remote_copy(
+            src_ref=source, dst_ref=target, send_sem=send, recv_sem=recv,
+            device_id={"tok": line * ROW + quarter}, device_id_type=MESH,
+        )
+
+    def rows(line, quarter):
+        return pl.ds(pl.multiple_of((line * ROW + quarter) * tokens, tokens), tokens)
+
+    def g_piece(line, quarter, piece):
+        columns = pl.ds(0, near) if piece == 0 else pl.ds(near, far)
+        return g_all.at[rows(line, quarter), columns]
+
+    def a_piece(line, quarter, number):
+        return a_all.at[rows(line, quarter), pl.ds(number * block, block)]
+
+    def arrived(ref, sem):
+        pltpu.make_async_copy(ref, ref, sem).wait()
+
+    def role(zz, part):
+        inner = zz in (1, 2)
+        mate = {0: 1, 1: 2, 2: 1, 3: 2}[zz]
+
+        def g_wait(line, quarter, piece):
+            arrived(g_piece(line, quarter, piece), g_recv.at[line, quarter, piece])
+
+        def g_forward(line, quarter, piece, target, send):
+            ref = g_piece(line, quarter, piece)
+            remote(ref, ref, send, g_recv.at[line, quarter, piece], target, s).start()
+
+        def a_wait(line, quarter, number):
+            arrived(a_piece(line, quarter, number), a_recv.at[line, quarter, number])
+
+        def a_forward(line, quarter, number, target, target_quarter, send):
+            ref = a_piece(line, quarter, number)
+            remote(ref, ref, send, a_recv.at[line, quarter, number], target, target_quarter).start()
+
+        def q_take(quarter):
+            held = pl.ds(pl.multiple_of(quarter * q_rows, q_rows), q_rows)
+            arrived(q_own.at[held, :], q_recv.at[quarter])
+            if not inner:
+                source = q_own.at[held, pl.ds(near, far)]
+                remote(source, q_next.at[held, :], n_send, n_recv.at[quarter], mate, s).start()
+
+        def spread(line):
+            for number in NEED[zz]:
+                for quarter in (core_peer, y_peer):
+                    a_forward(line, s, number, zz, quarter, act_row)
+
+        def relay(line):
+            for number in NEED[zz]:
+                a_wait(line, y_peer, number)
+                a_forward(line, y_peer, number, zz, core_peer, act_row)
+
+        def first(zz):
+            for place, quarter in enumerate(peers):
+                for piece in (0, 1):
+                    start = quarter * width + piece * near
+                    size = far if piece else near
+                    source = grads.at[:, pl.ds(pl.multiple_of(start, 128), size)]
+                    target = g_piece(zz, s, piece)
+                    sem = g_recv.at[zz, s, piece]
+                    if place == 0:
+                        pltpu.make_async_copy(source, target, sem).start()
+                    else:
+                        remote(source, target, row_send, sem, zz, quarter).start()
+            for number in NEED[zz]:
+                own = act.at[:, pl.ds(number * block, block)]
+                pltpu.make_async_copy(own, a_piece(zz, s, number), a_recv.at[zz, s, number]).start()
+            for target, numbers, send in (
+                (zz + 1, RIGHTWARD.get(zz + 1, ()), act_right), (zz - 1, LEFTWARD.get(zz - 1, ()), act_left),
+            ):
+                for number in numbers:
+                    own = act.at[:, pl.ds(number * block, block)]
+                    sem = a_recv.at[zz, s, number]
+                    remote(own, a_piece(zz, s, number), send, sem, target, s).start()
+
+            for quarter in peers:
+                g_wait(zz, quarter, 0)
+                if zz < LINE - 1:
+                    g_forward(zz, quarter, 0, zz + 1, right_a)
+                if zz > 0:
+                    g_forward(zz, quarter, 0, zz - 1, left_a)
+                g_wait(zz, quarter, 1)
+                g_forward(zz, quarter, 1, mate, right_b if zz < 2 else left_b)
+
+            for place, quarter in enumerate(peers):
+                start = pl.multiple_of(quarter * width, 128)
+                held = pl.ds(pl.multiple_of(s * q_rows, q_rows), q_rows)
+                source = query.at[:, pl.ds(start, width)]
+                target = q_own.at[held, :]
+                if place == 0:
+                    pltpu.make_async_copy(source, target, q_recv.at[s]).start()
+                else:
+                    remote(source, target, q_send, q_recv.at[s], zz, quarter).start()
+            for number in NEED[zz]:
+                a_wait(zz, s, number)
+            spread(zz)
+            for quarter in (s, core_peer):
+                q_take(quarter)
+
+        def drain(zz):
+            arrived(grads.at[:, pl.ds(0, 3 * width)], row_send)
+            arrived(query.at[:, pl.ds(0, 3 * width)], q_send)
+            line_rows = ROW * tokens
+            if zz < LINE - 1:
+                arrived(g_all.at[pl.ds(0, (zz + 1) * line_rows), pl.ds(0, near)], right_a)
+                wide = len(RIGHTWARD[zz + 1]) * block
+                arrived(a_all.at[pl.ds(0, (zz + 1) * tokens), pl.ds(0, wide)], act_right)
+            if zz > 0:
+                arrived(g_all.at[pl.ds(0, (LINE - zz) * line_rows), pl.ds(0, near)], left_a)
+                wide = len(LEFTWARD[zz - 1]) * block
+                arrived(a_all.at[pl.ds(0, (LINE - zz) * tokens), pl.ds(0, wide)], act_left)
+            half = g_all.at[pl.ds(0, (2 if inner else 1) * line_rows), pl.ds(near, far)]
+            arrived(half, right_b if zz < 2 else left_b)
+            if not inner:
+                arrived(q_next, n_send)
+            wide = len(NEED[zz]) * block
+            arrived(a_all.at[pl.ds(0, 3 * LINE * tokens), pl.ds(0, wide)], act_row)
+
+        last_line = LINE - 1 if zz < 2 else 0
+        last_distance = abs(last_line - zz)
+
+        def acts_in(distance):
+            from_left, from_right = zz - distance, zz + distance
+            if from_left >= 0:
+                for number in RIGHTWARD[zz]:
+                    a_wait(from_left, s, number)
+                for number in RIGHTWARD.get(zz + 1, ()):
+                    a_forward(from_left, s, number, zz + 1, s, act_right)
+                spread(from_left)
+            if from_right < LINE:
+                for number in LEFTWARD[zz]:
+                    a_wait(from_right, s, number)
+                for number in LEFTWARD.get(zz - 1, ()):
+                    a_forward(from_right, s, number, zz - 1, s, act_left)
+                spread(from_right)
+
+        def grads_in(distance, quarter):
+            from_left, from_right = zz - distance, zz + distance
+            if from_left >= 0:
+                g_wait(from_left, quarter, 0)
+                if zz < LINE - 1:
+                    g_forward(from_left, quarter, 0, zz + 1, right_a)
+            if from_right < LINE:
+                g_wait(from_right, quarter, 0)
+                if zz > 0:
+                    g_forward(from_right, quarter, 0, zz - 1, left_a)
+            if inner and from_left >= 0:
+                g_wait(from_left, quarter, 1)
+                if zz == 1:
+                    g_forward(from_left, quarter, 1, mate, right_b)
+            if inner and from_right < LINE:
+                g_wait(from_right, quarter, 1)
+                if zz == 2:
+                    g_forward(from_right, quarter, 1, mate, left_b)
+
+        def acts_ready(line):
+            for quarter in (core_peer, diagonal):
+                for number in NEED[zz]:
+                    a_wait(line, quarter, number)
+
+        if part == 0:
+            first(zz)
+            for distance in range(1, last_distance):
+                acts_in(distance)
+                for quarter in peers:
+                    grads_in(distance, quarter)
+                if distance == 1:
+                    for quarter in (y_peer, diagonal):
+                        q_take(quarter)
+                    relay(zz)
+                for line in (zz - distance, zz + distance):
+                    if 0 <= line < LINE:
+                        relay(line)
+            acts_in(last_distance)
+            for quarter in peers[:2]:
+                grads_in(last_distance, quarter)
+            for line in range(LINE):
+                if line != last_line:
+                    acts_ready(line)
+        elif part == 1:
+            grads_in(last_distance, peers[2])
+            relay(last_line)
+            if inner:
+                for quarter in range(ROW):
+                    held = pl.ds(quarter * q_rows, q_rows)
+                    arrived(q_next.at[held, :], n_recv.at[quarter])
+        elif part == 2:
+            grads_in(last_distance, peers[3])
+            acts_ready(last_line)
+        else:
+            drain(zz)
+
+    def run(part):
+        for zz in range(LINE):
+            pl.when(z == zz)(functools.partial(role, zz, part))
+
+    tall = 2 * tokens
+    tile = 512
+    is_inner = (z == 1) | (z == 2)
+    first_rows = pl.multiple_of((z // 2) * ROW * tokens, tokens)
+    last_rows = pl.multiple_of((1 - z // 2) * (LINE - 1) * ROW * tokens, tokens)
+    near_act = pl.ds(pl.multiple_of(z * block, block), block)
+    mate_line = z + 1 - 2 * (z % 2)
+    mate_act = pl.ds(pl.multiple_of(mate_line * block, block), block)
+
+    def add(held, projected, columns):
+        weighed = projected * g_all[held, columns].astype(jnp.float32)
+        parts = [weighed[:, i * 128 : (i + 1) * 128] for i in range(tile // 128)]
+        total[held, :] += sum(parts[1:], parts[0])
+
+    def near_block(start, count):
+        def step(number, carried):
+            held = pl.ds(pl.multiple_of(start + number % count * tall, tall), tall)
+            columns = pl.ds(pl.multiple_of(number // count * tile, tile), tile)
+            add(held, jnp.dot(
+                a_all[held, near_act], q_own[:, columns], preferred_element_type=jnp.float32
+            ), columns)
+            return carried
+
+        lax.fori_loop(0, near // tile * count, step, 0)
+
+    def far_block(start, count):
+        def step(number, carried):
+            held = pl.ds(pl.multiple_of(start + number % count * tall, tall), tall)
+            local = pl.multiple_of(number // count * tile, tile)
+            columns = pl.ds(pl.multiple_of(near + local, tile), tile)
+            projected = jnp.dot(
+                a_all[held, near_act], q_own[:, columns], preferred_element_type=jnp.float32
+            ) + jnp.dot(
+                a_all[held, mate_act], q_next[:, pl.ds(local, tile)],
+                preferred_element_type=jnp.float32,
+            )
+            add(held, projected, columns)
+            return carried
+
+        @pl.when(is_inner)
+        def _():
+            lax.fori_loop(0, far // tile * count, step, 0)
+
+    whole = (LINE - 1) * ROW // 2
+    total[...] = jnp.zeros_like(total)
+    run(0)
+    near_block(first_rows, whole)
+    run(1)
+    far_block(first_rows, whole)
+    early = pl.multiple_of(last_rows + y * tall, tall)
+    late = pl.multiple_of(last_rows + (1 - y) * tall, tall)
+    run(2)
+    near_block(early, 1)
+    far_block(early, 1)
+    near_block(late, 1)
+    far_block(late, 1)
+
+    token_scores = jnp.sum(total[...], axis=1, keepdims=True)
+    sums = jnp.sum(token_scores * member[...], axis=0, keepdims=True)
+    mine[...] = jnp.broadcast_to(sums, mine.shape)
+    slots[me] = mine[...]
+    for step in range(1, ROW * LINE):
+        other = (me + step) % (ROW * LINE)
+        pltpu.make_async_remote_copy(
+            src_ref=mine, dst_ref=slots.at[me], send_sem=sum_send, recv_sem=sum_recv.at[me],
+            device_id={"tok": other}, device_id_type=MESH,
+        ).start()
+    for step in range(1, ROW * LINE):
+        other = (me + step) % (ROW * LINE)
+        arrived(slots.at[other], sum_recv.at[other])
+    out[...] = jnp.sum(slots[...], axis=0)
+    arrived(slots.at[pl.ds(0, ROW * LINE - 1)], sum_send)
+    run(3)
+
+
+def on_line(activations, out_grads, query_grad, token_order, doc_ids):
+    tokens, features = activations.shape
+    columns = out_grads.shape[1]
+    width = columns // ROW
+    near = width * 4 // 7 // 256 * 256
+    far = width - near
+    q_rows = query_grad.shape[0]
+    count = ROW * LINE
+    position = lax.axis_index("tok")
+    dma = pltpu.SemaphoreType.DMA
+    examples = E_DEV * count
+    places = jnp.arange(examples, dtype=jnp.int32)
+    begin = jnp.sum((doc_ids[:, None] < places[None, :]).astype(jnp.int32), axis=0)
+    end = jnp.sum((doc_ids[:, None] <= places[None, :]).astype(jnp.int32), axis=0)
+    member = (token_order[:, None] >= begin[None, :]) & (token_order[:, None] < end[None, :])
+    member = jnp.pad(member.astype(jnp.float32), ((0, 0), (0, 128 - examples)))
+    vmem = pltpu.VMEM
+    sums = pl.pallas_call(
+        functools.partial(exchange, near),
+        out_shape=jax.ShapeDtypeStruct((8, 128), jnp.float32),
+        in_specs=[pl.BlockSpec(memory_space=pl.ANY)] * 3 + [pl.BlockSpec(memory_space=vmem)],
+        out_specs=pl.BlockSpec(memory_space=vmem),
+        scratch_shapes=[
+            vmem((count * tokens, width), jnp.bfloat16),
+            vmem((count * tokens, features), jnp.bfloat16),
+            vmem((ROW * q_rows, width), jnp.bfloat16),
+            vmem((ROW * q_rows, far), jnp.bfloat16),
+            vmem((count * tokens, 128), jnp.float32),
+            vmem((8, 128), jnp.float32),
+            vmem((count, 8, 128), jnp.float32),
+            dma((LINE, ROW, 2)), dma((LINE, ROW, LINE)), dma((ROW,)), dma((ROW,)),
+        ] + [dma] * 10 + [dma((count,)), dma],
+        compiler_params=pltpu.CompilerParams(
+            collective_id=0, has_side_effects=True, vmem_limit_bytes=56 * 2**20
+        ),
+        name="exchange",
+    )(activations, out_grads, query_grad, member)
+    return lax.dynamic_slice(sums[0], (E_DEV * position,), (E_DEV,))
 
 
 def from_partner(array, axis, bit):
@@ -98,6 +447,7 @@
         P("groups"),
         P("groups"),
     )
+    local = on_line if mesh.shape["tok"] == ROW * LINE else per_device
     return jax.shard_map(
-        per_device, mesh=mesh, in_specs=placed, out_specs=P(("groups", "tok")), check_vma=False
+        local, mesh=mesh, in_specs=placed, out_specs=P(("groups", "tok")), check_vma=False
     )

time: 585 us -> 229 us (0.39)
  waiting for transfers between devices: 444 us -> 0 us
  Pallas kernels: 0 us -> 225 us
  other arithmetic: 46.5 us -> 2.99 us
  blocking collectives: 33.1 us -> 0 us
  matrix products: 28.1 us -> 0 us
  local copies, waits for them, and re-layouts: 18.1 us -> 1.26 us
  starting transfers between devices: 13.8 us -> 0 us
    ppermute x10 -> x0, waiting for transfers between devices: 444 us -> none  [the longest x9 422 us: from_partner(): lax.ppermute(array, axis, [(i, i ^ 1 << bit) for i in range(lax.axis_size...]
    pallas_call x0 -> x1, Pallas kernels: none -> 225 us  [on_line(): pl.pallas_call(functools.partial(exchange, near), out_shape=jax.ShapeDtyp...]
    unnamed x1 -> x0, blocking collectives: 33.1 us -> none
    select_n x10 -> x0, other arithmetic: 29.8 us -> none  [the longest x5 17.2 us: order_rows(): higher = jnp.where(own_bit == 0, other_rows, own_rows)]
    dot_general x3 -> x0, matrix products: 28.1 us -> none  [the longest x2 27.7 us: accumulate(): jnp.dot(columns, query_piece, preferred_element_type=jnp.float32)]
    concatenate x7 -> x0, other arithmetic: 16.6 us -> none  [order_rows(): return jnp.concatenate([lower_half, higher], axis=0)]
    ppermute x10 -> x0, starting transfers between devices: 13.8 us -> none  [the longest x9 11.3 us: from_partner(): lax.ppermute(array, axis, [(i, i ^ 1 << bit) for i in range(lax.axis_size...]
    unnamed x56 -> x0, local copies, waits for them, and re-layouts: 7.75 us -> none
  transfers between devices with their start and end apart: 10 -> 0, of which waited for: 6 -> 0; matrix products, arithmetic and copies ran while one was open for 8% -> 0% of each run, Pallas kernels for 0% -> 0%
where the time goes in v2:
time: 229 us
  Pallas kernels  225 us (98%)
  other arithmetic  2.99 us (1%)
    pallas_call x1, Pallas kernels, on_line(): pl.pallas_call(functools.partial(exchange, near), out_shape=jax.ShapeDtyp...  225 us

profile of v2, /device:TPU:0, one launch (start us, length us, event | category | flops | bytes accessed | tf_op | source)
XLA Modules:
  0.0 229.0 jit_solution(4939919301430078740)
XLA Ops:
  0.0 0.9 convert_reduce_fusion.1
  0.9 1.0 compare_and_fusion
  1.9 1.1 pad_convert_fusion.member
  3.0 224.7 %exchange.1 = f32[8,128]{1,0:T(8,128)} custom-call(bf16[128,4096]{1,0:T(8,128)(2,1)} %act.1, bf16[128,14336]{1,0:T(8,128)(2,1)} %grads.1, bf16[256,14336]{1,0:T(8,128)(2,1)} %query.1, f32[2048,128]{1,0:T(8,128)} %pad_convert_fusion.member), custom_call_target="tpu_custom_call" | custom-call | tf_op jit(solution)/shard_map/exchange/pallas_call | solution.py:335
  227.7 0.7 slice.3
  228.4 0.6 dynamic-slice_bitcast_fusion

commit v3 on v2

--- a/solution.py
+++ b/solution.py
@@ -11,13 +11,14 @@
 ROW = 4
 LINE = 4
 MESH = pl.DeviceIdType.MESH
-NEED = ((0,), (0, 1), (2, 3), (3,))
-RIGHTWARD = {1: (0, 1, 2, 3), 2: (2, 3), 3: (3,)}
-LEFTWARD = {2: (0, 1, 2, 3), 1: (0, 1), 0: (0,)}
+SPAN = (1, 2, 2, 1)
+NEED = ((0,), (0,), (2,), (3,))
+RIGHTWARD = {1: (0, 2), 2: (2,), 3: (3,)}
+LEFTWARD = {2: (0, 2), 1: (0,), 0: (0,)}
 
 
 def exchange(
-    near, act, grads, query, member, out, g_all, a_all, q_own, q_next, total, mine, slots,
+    near, act, grads, query, order, docs, out, g_all, a_all, q_own, q_next, total, mine, slots, final,
     g_recv, a_recv, q_recv, n_recv, row_send, right_a, right_b, left_a, left_b, act_right, act_left,
     act_row, q_send, n_send,
     sum_recv, sum_send,
@@ -55,8 +56,8 @@
         columns = pl.ds(0, near) if piece == 0 else pl.ds(near, far)
         return g_all.at[rows(line, quarter), columns]
 
-    def a_piece(line, quarter, number):
-        return a_all.at[rows(line, quarter), pl.ds(number * block, block)]
+    def a_piece(line, quarter, number, target):
+        return a_all.at[rows(line, quarter), pl.ds(number * block, SPAN[target] * block)]
 
     def arrived(ref, sem):
         pltpu.make_async_copy(ref, ref, sem).wait()
@@ -73,18 +74,36 @@
             remote(ref, ref, send, g_recv.at[line, quarter, piece], target, s).start()
 
         def a_wait(line, quarter, number):
-            arrived(a_piece(line, quarter, number), a_recv.at[line, quarter, number])
+            arrived(a_piece(line, quarter, number, zz), a_recv.at[line, quarter, number])
 
         def a_forward(line, quarter, number, target, target_quarter, send):
-            ref = a_piece(line, quarter, number)
+            ref = a_piece(line, quarter, number, target)
             remote(ref, ref, send, a_recv.at[line, quarter, number], target, target_quarter).start()
 
-        def q_take(quarter):
+        def q_piece(quarter, piece):
             held = pl.ds(pl.multiple_of(quarter * q_rows, q_rows), q_rows)
-            arrived(q_own.at[held, :], q_recv.at[quarter])
-            if not inner:
-                source = q_own.at[held, pl.ds(near, far)]
-                remote(source, q_next.at[held, :], n_send, n_recv.at[quarter], mate, s).start()
+            return q_own.at[held, pl.ds(0, near) if piece == 0 else pl.ds(near, far)]
+
+        def q_give(places, piece):
+            for place in places:
+                quarter = peers[place]
+                start = pl.multiple_of(quarter * width + piece * near, 128)
+                source = query.at[:, pl.ds(start, far if piece else near)]
+                sem = q_recv.at[s, piece]
+                if place == 0:
+                    pltpu.make_async_copy(source, q_piece(s, piece), sem).start()
+                else:
+                    remote(source, q_piece(s, piece), q_send, sem, zz, quarter).start()
+
+        def q_take(places, piece):
+            for place in places:
+                quarter = peers[place]
+                arrived(q_piece(quarter, piece), q_recv.at[quarter, piece])
+                if piece and not inner:
+                    held = pl.ds(pl.multiple_of(quarter * q_rows, q_rows), q_rows)
+                    remote(
+                        q_piece(quarter, 1), q_next.at[held, :], n_send, n_recv.at[quarter], mate, s
+                    ).start()
 
         def spread(line):
             for number in NEED[zz]:
@@ -109,15 +128,15 @@
                     else:
                         remote(source, target, row_send, sem, zz, quarter).start()
             for number in NEED[zz]:
-                own = act.at[:, pl.ds(number * block, block)]
-                pltpu.make_async_copy(own, a_piece(zz, s, number), a_recv.at[zz, s, number]).start()
+                own = act.at[:, pl.ds(number * block, SPAN[zz] * block)]
+                pltpu.make_async_copy(own, a_piece(zz, s, number, zz), a_recv.at[zz, s, number]).start()
             for target, numbers, send in (
                 (zz + 1, RIGHTWARD.get(zz + 1, ()), act_right), (zz - 1, LEFTWARD.get(zz - 1, ()), act_left),
             ):
                 for number in numbers:
-                    own = act.at[:, pl.ds(number * block, block)]
+                    own = act.at[:, pl.ds(number * block, SPAN[target] * block)]
                     sem = a_recv.at[zz, s, number]
-                    remote(own, a_piece(zz, s, number), send, sem, target, s).start()
+                    remote(own, a_piece(zz, s, number, target), send, sem, target, s).start()
 
             for quarter in peers:
                 g_wait(zz, quarter, 0)
@@ -128,20 +147,9 @@
                 g_wait(zz, quarter, 1)
                 g_forward(zz, quarter, 1, mate, right_b if zz < 2 else left_b)
 
-            for place, quarter in enumerate(peers):
-                start = pl.multiple_of(quarter * width, 128)
-                held = pl.ds(pl.multiple_of(s * q_rows, q_rows), q_rows)
-                source = query.at[:, pl.ds(start, width)]
-                target = q_own.at[held, :]
-                if place == 0:
-                    pltpu.make_async_copy(source, target, q_recv.at[s]).start()
-                else:
-                    remote(source, target, q_send, q_recv.at[s], zz, quarter).start()
             for number in NEED[zz]:
                 a_wait(zz, s, number)
             spread(zz)
-            for quarter in (s, core_peer):
-                q_take(quarter)
 
         def drain(zz):
             arrived(grads.at[:, pl.ds(0, 3 * width)], row_send)
@@ -149,21 +157,21 @@
             line_rows = ROW * tokens
             if zz < LINE - 1:
                 arrived(g_all.at[pl.ds(0, (zz + 1) * line_rows), pl.ds(0, near)], right_a)
-                wide = len(RIGHTWARD[zz + 1]) * block
+                wide = len(RIGHTWARD[zz + 1]) * SPAN[zz + 1] * block
                 arrived(a_all.at[pl.ds(0, (zz + 1) * tokens), pl.ds(0, wide)], act_right)
             if zz > 0:
                 arrived(g_all.at[pl.ds(0, (LINE - zz) * line_rows), pl.ds(0, near)], left_a)
-                wide = len(LEFTWARD[zz - 1]) * block
+                wide = len(LEFTWARD[zz - 1]) * SPAN[zz - 1] * block
                 arrived(a_all.at[pl.ds(0, (LINE - zz) * tokens), pl.ds(0, wide)], act_left)
             half = g_all.at[pl.ds(0, (2 if inner else 1) * line_rows), pl.ds(near, far)]
             arrived(half, right_b if zz < 2 else left_b)
             if not inner:
                 arrived(q_next, n_send)
-            wide = len(NEED[zz]) * block
+            wide = SPAN[zz] * block
             arrived(a_all.at[pl.ds(0, 3 * LINE * tokens), pl.ds(0, wide)], act_row)
 
         last_line = LINE - 1 if zz < 2 else 0
-        last_distance = abs(last_line - zz)
+        outside = {1: 0, 2: 3}.get(zz, -1)
 
         def acts_in(distance):
             from_left, from_right = zz - distance, zz + distance
@@ -180,59 +188,75 @@
                     a_forward(from_right, s, number, zz - 1, s, act_left)
                 spread(from_right)
 
-        def grads_in(distance, quarter):
-            from_left, from_right = zz - distance, zz + distance
-            if from_left >= 0:
-                g_wait(from_left, quarter, 0)
-                if zz < LINE - 1:
-                    g_forward(from_left, quarter, 0, zz + 1, right_a)
-            if from_right < LINE:
-                g_wait(from_right, quarter, 0)
-                if zz > 0:
-                    g_forward(from_right, quarter, 0, zz - 1, left_a)
-            if inner and from_left >= 0:
-                g_wait(from_left, quarter, 1)
-                if zz == 1:
-                    g_forward(from_left, quarter, 1, mate, right_b)
-            if inner and from_right < LINE:
-                g_wait(from_right, quarter, 1)
-                if zz == 2:
-                    g_forward(from_right, quarter, 1, mate, left_b)
+        def grads_in(line, piece):
+            for quarter in peers:
+                g_wait(line, quarter, piece)
+                if piece == 0 and line < zz < LINE - 1:
+                    g_forward(line, quarter, 0, zz + 1, right_a)
+                if piece == 0 and line > zz > 0:
+                    g_forward(line, quarter, 0, zz - 1, left_a)
+                if piece == 1 and line == outside:
+                    g_forward(line, quarter, 1, mate, right_b if zz == 1 else left_b)
 
         def acts_ready(line):
             for quarter in (core_peer, diagonal):
                 for number in NEED[zz]:
                     a_wait(line, quarter, number)
 
+        early_lines = [line for line in range(LINE) if line != last_line]
         if part == 0:
             first(zz)
-            for distance in range(1, last_distance):
-                acts_in(distance)
-                for quarter in peers:
-                    grads_in(distance, quarter)
-                if distance == 1:
-                    for quarter in (y_peer, diagonal):
-                        q_take(quarter)
-                    relay(zz)
-                for line in (zz - distance, zz + distance):
-                    if 0 <= line < LINE:
-                        relay(line)
-            acts_in(last_distance)
-            for quarter in peers[:2]:
-                grads_in(last_distance, quarter)
-            for line in range(LINE):
-                if line != last_line:
-                    acts_ready(line)
+            if inner:
+                acts_in(1)
+                q_give((1, 2, 3, 0), 0)
+                q_give((1, 2, 3, 0), 1)
+                grads_in(outside, 0)
+                grads_in(mate, 0)
+                acts_in(2)
+                grads_in(outside, 1)
+                grads_in(last_line, 0)
+                relay(zz)
+                relay(mate)
+                relay(outside)
+                relay(last_line)
+                q_take((0, 1, 2, 3), 0)
+            else:
+                q_give((1, 2, 3, 0), 1)
+                q_give((1, 0), 0)
+                q_take((0, 1), 1)
+                acts_in(1)
+                q_take((2, 3), 1)
+                q_give((2, 3), 0)
+                relay(zz)
+                grads_in(mate, 0)
+                relay(mate)
+                acts_in(2)
+                grads_in(3 - mate, 0)
+                relay(3 - mate)
+                acts_in(3)
+                q_take((0, 1, 2, 3), 0)
+            for line in early_lines:
+                acts_ready(line)
         elif part == 1:
-            grads_in(last_distance, peers[2])
-            relay(last_line)
+            if not inner:
+                grads_in(last_line, 0)
+                relay(last_line)
+            acts_ready(last_line)
+        elif part == 2:
             if inner:
+                q_take((0, 1, 2, 3), 1)
+                grads_in(mate, 1)
                 for quarter in range(ROW):
                     held = pl.ds(quarter * q_rows, q_rows)
                     arrived(q_next.at[held, :], n_recv.at[quarter])
-        elif part == 2:
-            grads_in(last_distance, peers[3])
-            acts_ready(last_line)
+        elif part == 3:
+            if inner:
+                for quarter in peers[:2]:
+                    g_wait(last_line, quarter, 1)
+        elif part == 4:
+            if inner:
+                for quarter in peers[2:]:
+                    g_wait(last_line, quarter, 1)
         else:
             drain(zz)
 
@@ -284,21 +308,38 @@
             lax.fori_loop(0, far // tile * count, step, 0)
 
     whole = (LINE - 1) * ROW // 2
+    early = pl.multiple_of(last_rows + y * tall, tall)
+    late = pl.multiple_of(last_rows + (1 - y) * tall, tall)
+    run(0)
     total[...] = jnp.zeros_like(total)
-    run(0)
     near_block(first_rows, whole)
     run(1)
+    near_block(last_rows, 2)
+    run(2)
     far_block(first_rows, whole)
-    early = pl.multiple_of(last_rows + y * tall, tall)
-    late = pl.multiple_of(last_rows + (1 - y) * tall, tall)
-    run(2)
-    near_block(early, 1)
+    examples = mine.shape[0]
+    numbers = lax.broadcasted_iota(jnp.int32, (examples, order.shape[1]), 0)
+    begin = jnp.sum((docs[...] < numbers).astype(jnp.int32), axis=1, keepdims=True)
+    end = jnp.sum((docs[...] <= numbers).astype(jnp.int32), axis=1, keepdims=True)
+
+    def example_sums(start, size):
+        held = pl.ds(start, size)
+        scores = lax.dot_general(
+            jnp.ones((8, 128), jnp.float32), total[held, :], (((1,), (1,)), ((), ())),
+            precision=lax.Precision.HIGHEST, preferred_element_type=jnp.float32,
+        )[0:1, :]
+        place = order[:, held]
+        member = (place >= begin) & (place < end)
+        return jnp.sum(jnp.where(member, scores, 0.0), axis=1, keepdims=True)
+
+    sums = example_sums(first_rows, whole * tall)
+    run(3)
     far_block(early, 1)
-    near_block(late, 1)
+    sums = sums + example_sums(early, tall)
+    run(4)
     far_block(late, 1)
-
-    token_scores = jnp.sum(total[...], axis=1, keepdims=True)
-    sums = jnp.sum(token_scores * member[...], axis=0, keepdims=True)
+    sums = sums + example_sums(late, tall)
+
     mine[...] = jnp.broadcast_to(sums, mine.shape)
     slots[me] = mine[...]
     for step in range(1, ROW * LINE):
@@ -310,9 +351,11 @@
     for step in range(1, ROW * LINE):
         other = (me + step) % (ROW * LINE)
         arrived(slots.at[other], sum_recv.at[other])
-    out[...] = jnp.sum(slots[...], axis=0)
+    mine_sum = jnp.sum(slots[...], axis=0)
+    final[...] = mine_sum
+    out[...] = final[pl.ds(E_DEV * me, E_DEV), :]
     arrived(slots.at[pl.ds(0, ROW * LINE - 1)], sum_send)
-    run(3)
+    run(5)
 
 
 def on_line(activations, out_grads, query_grad, token_order, doc_ids):
@@ -323,19 +366,13 @@
     far = width - near
     q_rows = query_grad.shape[0]
     count = ROW * LINE
-    position = lax.axis_index("tok")
     dma = pltpu.SemaphoreType.DMA
     examples = E_DEV * count
-    places = jnp.arange(examples, dtype=jnp.int32)
-    begin = jnp.sum((doc_ids[:, None] < places[None, :]).astype(jnp.int32), axis=0)
-    end = jnp.sum((doc_ids[:, None] <= places[None, :]).astype(jnp.int32), axis=0)
-    member = (token_order[:, None] >= begin[None, :]) & (token_order[:, None] < end[None, :])
-    member = jnp.pad(member.astype(jnp.float32), ((0, 0), (0, 128 - examples)))
     vmem = pltpu.VMEM
     sums = pl.pallas_call(
         functools.partial(exchange, near),
-        out_shape=jax.ShapeDtypeStruct((8, 128), jnp.float32),
-        in_specs=[pl.BlockSpec(memory_space=pl.ANY)] * 3 + [pl.BlockSpec(memory_space=vmem)],
+        out_shape=jax.ShapeDtypeStruct((E_DEV, 128), jnp.float32),
+        in_specs=[pl.BlockSpec(memory_space=pl.ANY)] * 3 + [pl.BlockSpec(memory_space=vmem)] * 2,
         out_specs=pl.BlockSpec(memory_space=vmem),
         scratch_shapes=[
             vmem((count * tokens, width), jnp.bfloat16),
@@ -343,16 +380,19 @@
             vmem((ROW * q_rows, width), jnp.bfloat16),
             vmem((ROW * q_rows, far), jnp.bfloat16),
             vmem((count * tokens, 128), jnp.float32),
-            vmem((8, 128), jnp.float32),
-            vmem((count, 8, 128), jnp.float32),
-            dma((LINE, ROW, 2)), dma((LINE, ROW, LINE)), dma((ROW,)), dma((ROW,)),
+            vmem((examples, 128), jnp.float32),
+            vmem((count, examples, 128), jnp.float32),
+            vmem((examples, 128), jnp.float32),
+            dma((LINE, ROW, 2)), dma((LINE, ROW, LINE)), dma((ROW, 2)), dma((ROW,)),
         ] + [dma] * 10 + [dma((count,)), dma],
         compiler_params=pltpu.CompilerParams(
             collective_id=0, has_side_effects=True, vmem_limit_bytes=56 * 2**20
         ),
         name="exchange",
-    )(activations, out_grads, query_grad, member)
-    return lax.dynamic_slice(sums[0], (E_DEV * position,), (E_DEV,))
+    )(
+        activations, out_grads, query_grad, token_order.reshape(1, -1), doc_ids.reshape(1, -1)
+    )
+    return sums[:, 0]
 
 
 def from_partner(array, axis, bit):

time: 229 us -> 214 us (0.934)
  Pallas kernels: 225 us -> 212 us
  other arithmetic: 2.99 us -> 0 us
    pallas_call x1, Pallas kernels: 225 us -> 212 us  [on_line(): pl.pallas_call(functools.partial(exchange, near), out_shape=jax.ShapeDtyp...]
where the time goes in v3:
time: 214 us
  Pallas kernels  212 us (99%)
    pallas_call x1, Pallas kernels, on_line(): pl.pallas_call(functools.partial(exchange, near), out_shape=jax.ShapeDtyp...  212 us

profile of v3, /device:TPU:0, one launch (start us, length us, event | category | flops | bytes accessed | tf_op | source)
XLA Modules:
  0.0 213.5 jit_solution(14067530144891168903)
XLA Ops:
  0.0 212.2 %exchange.1 = f32[2,128]{1,0:T(2,128)} custom-call(bf16[128,4096]{1,0:T(8,128)(2,1)} %act.1, bf16[128,14336]{1,0:T(8,128)(2,1)} %grads.1, bf16[256,14336]{1,0:T(8,128)(2,1)} %query.1, s32[1,2048]{1,0:T(1,128)} %bitcast.2, s32[1,2048]{1,0:T(1,128)} %bitcast.3), custom_call_target="tpu_custom_call" | custom-call | tf_op jit(solution)/shard_map/exchange/pallas_call | solution.py:372
  212.2 1.3 slice_reduce_fusion

commit v4 on v3

--- a/solution.py
+++ b/solution.py
@@ -138,7 +138,13 @@
                     sem = a_recv.at[zz, s, number]
                     remote(own, a_piece(zz, s, number, target), send, sem, target, s).start()
 
-            for quarter in peers:
+            home(peers[:2])
+            for number in NEED[zz]:
+                a_wait(zz, s, number)
+            spread(zz)
+
+        def home(quarters):
+            for quarter in quarters:
                 g_wait(zz, quarter, 0)
                 if zz < LINE - 1:
                     g_forward(zz, quarter, 0, zz + 1, right_a)
@@ -146,10 +152,6 @@
                     g_forward(zz, quarter, 0, zz - 1, left_a)
                 g_wait(zz, quarter, 1)
                 g_forward(zz, quarter, 1, mate, right_b if zz < 2 else left_b)
-
-            for number in NEED[zz]:
-                a_wait(zz, s, number)
-            spread(zz)
 
         def drain(zz):
             arrived(grads.at[:, pl.ds(0, 3 * width)], row_send)
@@ -188,8 +190,8 @@
                     a_forward(from_right, s, number, zz - 1, s, act_left)
                 spread(from_right)
 
-        def grads_in(line, piece):
-            for quarter in peers:
+        def grads_in(line, piece, quarters=peers):
+            for quarter in quarters:
                 g_wait(line, quarter, piece)
                 if piece == 0 and line < zz < LINE - 1:
                     g_forward(line, quarter, 0, zz + 1, right_a)
@@ -206,13 +208,15 @@
         early_lines = [line for line in range(LINE) if line != last_line]
         if part == 0:
             first(zz)
+            acts_in(1)
+            home(peers[2:])
             if inner:
-                acts_in(1)
                 q_give((1, 2, 3, 0), 0)
+                acts_in(2)
                 q_give((1, 2, 3, 0), 1)
-                grads_in(outside, 0)
-                grads_in(mate, 0)
-                acts_in(2)
+                for quarter in peers:
+                    grads_in(mate, 0, (quarter,))
+                    grads_in(outside, 0, (quarter,))
                 grads_in(outside, 1)
                 grads_in(last_line, 0)
                 relay(zz)
@@ -224,16 +228,15 @@
                 q_give((1, 2, 3, 0), 1)
                 q_give((1, 0), 0)
                 q_take((0, 1), 1)
-                acts_in(1)
                 q_take((2, 3), 1)
+                acts_in(2)
                 q_give((2, 3), 0)
                 relay(zz)
+                acts_in(3)
                 grads_in(mate, 0)
                 relay(mate)
-                acts_in(2)
                 grads_in(3 - mate, 0)
                 relay(3 - mate)
-                acts_in(3)
                 q_take((0, 1, 2, 3), 0)
             for line in early_lines:
                 acts_ready(line)

time: 214 us -> 203 us (0.949)
  Pallas kernels: 212 us -> 201 us
    pallas_call x1, Pallas kernels: 212 us -> 201 us  [on_line(): pl.pallas_call(functools.partial(exchange, near), out_shape=jax.ShapeDtyp...]
where the time goes in v4:
time: 203 us
  Pallas kernels  201 us (99%)
    pallas_call x1, Pallas kernels, on_line(): pl.pallas_call(functools.partial(exchange, near), out_shape=jax.ShapeDtyp...  201 us

profile of v4, /device:TPU:0, one launch (start us, length us, event | category | flops | bytes accessed | tf_op | source)
XLA Modules:
  0.0 202.5 jit_solution(8995780433485688966)
XLA Ops:
  0.0 201.2 %exchange.1 = f32[2,128]{1,0:T(2,128)} custom-call(bf16[128,4096]{1,0:T(8,128)(2,1)} %act.1, bf16[128,14336]{1,0:T(8,128)(2,1)} %grads.1, bf16[256,14336]{1,0:T(8,128)(2,1)} %query.1, s32[1,2048]{1,0:T(1,128)} %bitcast.2, s32[1,2048]{1,0:T(1,128)} %bitcast.3), custom_call_target="tpu_custom_call" | custom-call | tf_op jit(solution)/shard_map/exchange/pallas_call | solution.py:375
  201.2 1.3 slice_reduce_fusion
